TPU v7x, 32 devices: a whole 2x2x4 slice. The times are simulated.
32 devices in a mesh: leaf: 2 (over y), row: 2 (over x), col: 8 (over z, core).
Axes of the slice: x: 2, y: 2, z: 4, core: 2. Of those that a mesh axis runs over, the one named last changes fastest.
Arguments:
- front_window: float32 [49152, 2048], P(('leaf', 'row'), 'col'), parts along dimension 0, may hold values from -8 to 785
- children: float32 [65536, 2048], P(('leaf', 'row', 'col')), parts along dimension 0, may hold values from -1 to 1
- row_map: int32 [4, 128], P('leaf'), parts along dimension 0, may hold values from 0 to 191, as said below
- col_map: int32 [4, 16], P('leaf'), parts along dimension 0, may hold values from 0 to 15, as said below
Outputs:
- factored: float32 [49152, 2048], P(('leaf', 'row'), 'col'), parts along dimension 0
There are 2 independent parts, one for each index of `leaf`. A program takes and returns all parts, laid end to end along the dimension named above; each array names one. Nothing has to cross between parts.
Inputs may be any that keep to these rules, and one draw needn't show every extreme that they name: `row_map`: for each sibling, its entries are distinct; each aligned run of 128 of its row blocks names exactly 64 blocks in each range of 96 consecutive parent blocks. `col_map`: each sibling's row is a permutation of the 16 window blocks.
All inputs are finite; a program needn't handle non-finite values.
Results may differ from a plain program's by a relative error of at most 0.000088.
Values sent between devices are 32-bit elements; how exact they have to be, the bound alone decides.
A program may use at most 192 MiB of HBM per device.

v0:
```python
import jax
import jax.numpy as jnp
from jax import lax
from jax.sharding import PartitionSpec as P

BLK = 128
PANEL = 256


def broadcast(value, axis, source):
    kept = jnp.where(lax.axis_index(axis) == source, value, 0).astype(value.dtype)
    return lax.psum(kept, axis)


def body(front_window, children, row_map, col_map):
    row_count = lax.axis_size("row")
    col_count = lax.axis_size("col")
    row_index = lax.axis_index("row")
    col_index = lax.axis_index("col")
    rows_here, cols_here = front_window.shape
    child_rows = children.shape[0]
    window_blocks = children.shape[1] // BLK
    sibling = row_index // (row_count // 2)
    chosen_cols = lax.dynamic_index_in_dim(col_map, sibling, 0, keepdims=False)
    inverse_cols = jnp.argsort(chosen_cols)
    spread = jnp.take(children.reshape(child_rows, window_blocks, BLK), inverse_cols, axis=1)
    spread = spread.reshape(child_rows, col_count, cols_here)
    quarter = lax.all_to_all(spread, "col", split_axis=1, concat_axis=0, tiled=True)
    quarter = quarter.reshape(col_count * child_rows, cols_here)
    quarter_blocks = quarter.shape[0] // BLK
    capacity = quarter_blocks // row_count
    parent_blocks = rows_here // BLK
    source_maps = row_map.reshape(row_count, quarter_blocks)
    owners = source_maps // parent_blocks
    ordering = jnp.argsort(owners, axis=1, stable=True)
    own_order = lax.dynamic_index_in_dim(ordering, row_index, 0, keepdims=False)
    outgoing = jnp.take(quarter.reshape(quarter_blocks, BLK, cols_here), own_order, axis=0)
    outgoing = outgoing.reshape(row_count, capacity * BLK, cols_here)
    incoming = lax.all_to_all(outgoing, "row", split_axis=0, concat_axis=0, tiled=True)
    chosen = lax.dynamic_slice_in_dim(ordering, row_index * capacity, capacity, axis=1)
    targets = (jnp.take_along_axis(source_maps, chosen, axis=1) % parent_blocks).reshape(-1)
    selector = (targets[:, None] == jnp.arange(parent_blocks, dtype=jnp.int32)[None, :]).astype(
        jnp.float32
    )
    added = jnp.einsum(
        "sp,sk->pk",
        selector,
        incoming.reshape(row_count * capacity, BLK * cols_here),
        precision=lax.Precision.HIGHEST,
    )
    assembled = front_window + added.reshape(rows_here, cols_here)
    identity = jnp.eye(PANEL, dtype=jnp.float32)
    global_rows = row_index * rows_here + jnp.arange(rows_here, dtype=jnp.int32)
    panel_rows = broadcast(assembled, "col", 0)
    diagonal_block = broadcast(panel_rows[:PANEL], "row", 0)
    factor = jnp.linalg.cholesky(diagonal_block)
    inverse = jax.scipy.linalg.solve_triangular(factor, identity, lower=True)
    solved = jnp.dot(panel_rows, inverse.T, precision=lax.Precision.HIGHEST)
    leading = jnp.where(row_index == 0, factor, solved[:PANEL])
    lower_panel = jnp.concatenate([leading, solved[PANEL:]], axis=0)
    owner_row = col_index * cols_here // rows_here
    start = jnp.clip(col_index * cols_here - row_index * rows_here, 0, rows_here - cols_here)
    piece = lax.dynamic_slice_in_dim(lower_panel, start, cols_here, 0)
    matching = broadcast(piece, "row", owner_row)
    update = jnp.dot(lower_panel, matching.T, precision=lax.Precision.HIGHEST)
    global_cols = col_index * cols_here + jnp.arange(cols_here, dtype=jnp.int32)
    inside = (global_rows >= PANEL)[:, None] & (global_cols >= PANEL)[None, :]
    result = jnp.where(inside, assembled - update, assembled)
    return jnp.where((global_cols < PANEL)[None, :], lower_panel, result)


def solution(mesh):
    placed = (
        P(("leaf", "row"), "col"),
        P(("leaf", "row", "col"), None),
        P("leaf", None),
        P("leaf", None),
    )
    return jax.shard_map(
        body, mesh=mesh, in_specs=placed, out_specs=P(("leaf", "row"), "col"), check_vma=False
    )
```

profile of v0, /device:TPU:0, one launch (start us, length us, event | category | flops | bytes accessed | tf_op | source)
XLA Modules:
  0.0 1209.6 jit_solution(6401520857214902791)
XLA Ops:
  8.5 17.6 %copy.29 = f32[2048,2048]{0,1:T(8,128)} copy(f32[2048,2048]{1,0:T(8,128)} %param.5) | data formatting | bytes 33554432 | tf_op args[1]
  26.1 17.6 %copy.30 = f32[2048,16,128]{2,0,1:T(8,128)} copy(f32[2048,16,128]{0,2,1:T(8,128)} %bitcast.65) | data formatting | bytes 33554432 | tf_op jit(solution)/shard_map/reshape | solution.py:26
  43.7 13.8 %gather_fusion = f32[16,2048,128]{2,1,0:T(8,128)} fusion(f32[2048,16,128]{2,0,1:T(8,128)} %copy.30, s32[1024]{0:T(1024)S(1)} %pad_clamp_fusion.1), kind=kCustom, calls=%fused_computation | custom fusion | bytes 33554496 | tf_op jit(solution)/shard_map/jit(_take)/gather | solution.py:26
  57.5 17.6 %copy.31 = f32[2048,16,128]{0,2,1:T(8,128)} copy(f32[2048,16,128]{2,0,1:T(8,128)} %bitcast.63) | data formatting | bytes 33554432 | tf_op jit(solution)/shard_map/jit(_take)/gather | solution.py:26
  75.4 11.4 bitcast_select_fusion.1
  86.8 6.5 all-to-all-start
  94.5 4.2 sort.37.cloned.1.call-done
  100.2 356.8 %all-to-all-done = f32[2048,8,256]{0,2,1:T(8,128)} async-done(((f32[2048,8,256]{0,2,1:T(8,128)}), f32[2048,8,256]{0,2,1:T(8,128)}, u32[]{:S(2)}, u32[]{:S(2)}) %all-to-all-start) | async-done | bytes 16777248 | tf_op jit(solution)/shard_map/all_to_all | solution.py:28
  457.1 16.4 %copy.32 = f32[8,2048,1,256]{3,1,0,2:T(8,128)} copy(f32[8,2048,1,256]{1,3,0,2:T(8,128)} %bitcast.7) | data formatting | bytes 33554432 | tf_op jit(solution)/shard_map/all_to_all | solution.py:28
  473.5 15.6 %gather_fusion.1 = f32[128,128,256]{2,1,0:T(8,128)} fusion(f32[128,128,256]{2,1,0:T(8,128)} %bitcast.64, s32[1024]{0:T(1024)S(1)} %pad_clamp_fusion), kind=kCustom, calls=%fused_computation.1 | custom fusion | bytes 33554944 | tf_op jit(solution)/shard_map/jit(_take)/gather | solution.py:37
  489.1 12.2 %bitcast_select_fusion = f32[2,8192,256]{2,1,0:T(8,128)} fusion(pred[2,8192]{1,0:T(4,128)(4,1)S(1)} %bitcast.66, f32[2,8192,256]{2,1,0:T(8,128)} %bitcast.61), kind=kLoop, calls=%fused_computation.8 | loop fusion | flops 4194304 | bytes 33570816 | tf_op jit(solution)/shard_map/jit(_take)/select_n | solution.py:37
  501.3 9.7 all-to-all-start.1
  511.4 12.6 %copy.33 = f32[12288,256]{0,1:T(8,128)} copy(f32[12288,256]{1,0:T(8,128)} %param.4) | data formatting | bytes 25165824 | tf_op args[0]
  525.9 167.8 %all-to-all-done.1 = f32[2,8192,256]{2,1,0:T(8,128)} async-done(((f32[2,8192,256]{2,1,0:T(8,128)}), f32[2,8192,256]{2,1,0:T(8,128)}, u32[]{:S(2)}, u32[]{:S(2)}) %all-to-all-start.1) | async-done | bytes 16777248 | tf_op jit(solution)/shard_map/all_to_all | solution.py:39
  693.7 18.2 %reshape.123 = f32[128,32768]{1,0:T(8,128)} reshape(f32[2,8192,256]{2,1,0:T(8,128)} %all-to-all-done.1) | data formatting | bytes 33554432 | tf_op jit(solution)/shard_map/reshape | solution.py:48
  712.0 14.2 %fusion.17 = f32[96,32768]{1,0:T(8,128)} fusion(f32[128,32768]{1,0:T(8,128)} %reshape.123, s32[128]{0:T(128)S(1)} %and_select_fusion), kind=kOutput, calls=%fused_computation.46 | convolution fusion | flops 4831850496 | bytes 29360640 | tf_op jit(solution)/shard_map/sp,sk->pk/dot_general | solution.py:45
  726.2 13.6 %reshape.124 = f32[12288,256]{1,0:T(8,128)} reshape(f32[96,32768]{1,0:T(8,128)} %fusion.17) | data formatting | bytes 25165824 | tf_op jit(solution)/shard_map/reshape | solution.py:51
  739.8 12.6 %copy.34 = f32[12288,256]{0,1:T(8,128)} copy(f32[12288,256]{1,0:T(8,128)} %reshape.124) | data formatting | bytes 25165824 | tf_op jit(solution)/shard_map/reshape | solution.py:51
  752.4 18.5 %broadcast_select_fusion = (f32[12288,256]{0,1:T(8,128)}, f32[12288,256]{0,1:T(8,128)}) fusion(pred[]{:T(512)S(6)} %eq.31, f32[12288,256]{0,1:T(8,128)} %copy.33, f32[12288,256]{0,1:T(8,128)} %copy.34), kind=kLoop, calls=%fused_computation.13 | loop fusion | flops 6291456 | bytes 50331648 | tf_op jit(solution)/shard_map/jit(_where)/select_n | solution.py:11
  771.0 253.3 %all-reduce.5.cloned.1.call-done = f32[12288,256]{0,1:T(8,128)} async-done(((f32[12288,256]{0,1:T(8,128)}), f32[12288,256]{0,1:T(8,128)}) %all-reduce.5.cloned.1.call-update) | async-done | bytes 12582928 | tf_op jit(solution)/shard_map/psum | solution.py:12
  1026.7 23.4 %all-reduce.7.cloned.1.call-done = f32[256,256]{0,1:T(8,128)} async-done(((f32[256,256]{0,1:T(8,128)}), f32[256,256]{0,1:T(8,128)}) %all-reduce.7.cloned.1.call-update) | async-done | bytes 262160 | tf_op jit(solution)/shard_map/psum | solution.py:12
  1052.3 11.7 cholesky.49
  1064.0 9.8 custom-call.15
  1074.3 11.7 cholesky.103
  1088.5 4.3 while.1
  1092.8 19.7 %custom-call.16 = f32[2,128,128]{1,2,0:T(8,128)S(1)} custom-call(f32[2,128,128]{2,1,0:T(8,128)S(1)} %get-tuple-element.16), custom_call_target="InvertDiagBlocksLowerTriangular" | custom-call | tf_op jit(solution)/shard_map/jit(_solve_triangular)/triangular_solve | solution.py:57
  1113.3 14.1 %fusion.3 = f32[12288,256]{0,1:T(8,128)S(1)} fusion(f32[12288,256]{0,1:T(8,128)} %all-reduce.5.cloned.1.call-done, f32[128,256]{1,0:T(8,128)S(1)} %fusion.13, f32[128,256]{1,0:T(8,128)S(1)} %fusion.10), kind=kOutput, calls=%fused_computation.19 | convolution fusion | flops 9663741952 | bytes 25427968 | tf_op jit(solution)/shard_map/dot_general | solution.py:58
  1127.5 4.8 copy-done.3
  1132.3 9.7 slice.79
  1143.8 23.4 %all-reduce.9.cloned.1.call-done = f32[256,256]{0,1:T(8,128)} async-done(((f32[256,256]{0,1:T(8,128)}), f32[256,256]{0,1:T(8,128)}) %all-reduce.9.cloned.1.call-update) | async-done | bytes 262160 | tf_op jit(solution)/shard_map/psum | solution.py:12
  1167.2 23.0 %fusion = f32[12288,256]{0,1:T(8,128)} fusion(f32[12288,256]{0,1:T(8,128)} %get-tuple-element.38, f32[256,256]{0,1:T(8,128)} %all-reduce.9.cloned.1.call-done, f32[256,256]{0,1:T(8,128)S(1)} %slice_select_fusion, f32[12032,256]{0,1:T(8,128)} %slice.79, pred[256]{0:T(512)(128)(4,1)S(1)} %get-tuple-element.44, pred[12288]{0:T(1024)(128)(4,1)S(1)} %add_compare_fusion, ...), kind=kOutput, calls=%fused_computation.10 | convolution fusion | flops 9682550784 | bytes 38023680 | tf_op jit(solution)/shard_map/dot_general | solution.py:65
  1190.2 12.6 %copy.43 = f32[12288,256]{1,0:T(8,128)} copy(f32[12288,256]{0,1:T(8,128)} %fusion) | data formatting | bytes 25165824 | tf_op jit(solution)/shard_map/jit(_where)/select_n | solution.py:69
  (79 shorter events, 20.2 us)
Async XLA Ops:
  6.5 0.7 copy-start
  86.8 6.5 copy-start.2
  86.8 370.3 %all-to-all-start = ((f32[2048,8,256]{0,2,1:T(8,128)}), f32[2048,8,256]{0,2,1:T(8,128)}, u32[]{:S(2)}, u32[]{:S(2)}) async-start(f32[2048,8,256]{0,2,1:T(8,128)} %bitcast_select_fusion.1), calls=%async_computation | async-start | bytes 33554432 | tf_op jit(solution)/shard_map/all_to_all | solution.py:28
  93.2 5.4 sort.37.cloned.1.call-start
  501.3 192.4 %all-to-all-start.1 = ((f32[2,8192,256]{2,1,0:T(8,128)}), f32[2,8192,256]{2,1,0:T(8,128)}, u32[]{:S(2)}, u32[]{:S(2)}) async-start(f32[2,8192,256]{2,1,0:T(8,128)} %bitcast_select_fusion), calls=%async_computation.1 | async-start | bytes 33554432 | tf_op jit(solution)/shard_map/all_to_all | solution.py:39
  511.0 513.4 %all-reduce.5.cloned.1.call-start = ((), (), s32[]{:S(2)}) async-start(), calls=%async_computation.2 | async-start | bytes 25165824 | tf_op jit(solution)/shard_map/psum | solution.py:12
  511.4 12.6 %copy-start.4 = (s32[2,128]{1,0:T(2,128)S(1)}, s32[2,128]{1,0:T(2,128)}, u32[]{:S(2)}) copy-start(s32[2,128]{1,0:T(2,128)} %get-tuple-element.7) | copy-start | bytes 3076
  771.0 279.2 %all-reduce.7.cloned.1.call-start = ((), (), s32[]{:S(2)}) async-start(), calls=%async_computation.3 | async-start | bytes 524288 | tf_op jit(solution)/shard_map/psum | solution.py:12
  1026.1 141.2 %all-reduce.9.cloned.1.call-start = ((), (), s32[]{:S(2)}) async-start(), calls=%async_computation.4 | async-start | bytes 524288 | tf_op jit(solution)/shard_map/psum | solution.py:12
  1127.5 4.8 copy-start.3
  1167.2 35.6 %copy-start.1 = (s32[2,16]{1,0:T(2,128)S(1)}, s32[2,16]{1,0:T(2,128)}, u32[]{:S(2)}) copy-start(s32[2,16]{1,0:T(2,128)} %param.7) | copy-start | bytes 388
Sparse Core Ops, SparseCore 0:
  96.3 2.0 sort.39.cloned.1.call-done
  771.1 253.2 all-reduce.4
  1026.7 23.3 all-reduce.6
  1143.9 23.2 all-reduce.8
  (1 shorter events, 0.0 us)
where the time goes:
time: 1220 us; the launch traced here: 1210 us
  waiting for transfers between devices  825 us (68%)
  local copies, waits for them, and re-layouts  197 us (16%)
  other arithmetic  103 us (8%)
  matrix products  52.6 us (4%)
  starting transfers between devices  17.1 us (1%)
  between operations  14.9 us (1%)
    all_to_all x1, waiting for transfers between devices, body(): lax.all_to_all(spread, 'col', split_axis=1, concat_axis=0, tiled=True)  357 us
    psum x3, waiting for transfers between devices, broadcast(): return lax.psum(kept, axis)  300 us
    all_to_all x1, waiting for transfers between devices, body(): lax.all_to_all(outgoing, 'row', split_axis=0, concat_axis=0, tiled=True)  168 us
    unnamed x15, local copies, waits for them, and re-layouts  35.8 us
    another operation x6, other arithmetic, body(): factor = jnp.linalg.cholesky(diagonal_block)  34 us
    gather x2, local copies, waits for them, and re-layouts, body(): jnp.take(children.reshape(child_rows, window_blocks, BLK), inverse_cols,...  31.4 us
    reshape x2, local copies, waits for them, and re-layouts, body(): assembled = front_window + added.reshape(rows_here, cols_here)  26.2 us
  transfers between devices with their start and end apart: 5, of which 5 were waited for; matrix products, arithmetic and copies ran while one was open for 1% of the time, Pallas kernels for 0%

commit v1 on v0

--- a/solution.py
+++ b/solution.py
@@ -5,6 +5,25 @@
 
 BLK = 128
 PANEL = 256
+
+
+def _spread_ports(z_in, mesh_name, ndim_at, k_dim):
+    carry = lax.psum(1, mesh_name)
+    reached = lax.axis_index(mesh_name)
+    finding, z2 = (carry, reached)
+    k_now = z_in.shape[ndim_at] // finding
+    e_next = list(z_in.shape)
+    e_next[ndim_at] = k_now
+    state_now = e_next[k_dim]
+    e_next[k_dim] = state_now * finding
+    heard = jnp.zeros(e_next, z_in.dtype)
+    for t in range(finding):
+        front = lax.dynamic_slice_in_dim(z_in, (z2 ^ t) * k_now, k_now, axis=ndim_at)
+        if t:
+            val2 = tuple(((q, q ^ t) for q in range(finding)))
+            front = lax.ppermute(front, mesh_name, val2)
+        heard = lax.dynamic_update_slice_in_dim(heard, front, (z2 ^ t) * state_now, axis=k_dim)
+    return heard
 
 
 def broadcast(value, axis, source):
@@ -25,7 +44,7 @@
     inverse_cols = jnp.argsort(chosen_cols)
     spread = jnp.take(children.reshape(child_rows, window_blocks, BLK), inverse_cols, axis=1)
     spread = spread.reshape(child_rows, col_count, cols_here)
-    quarter = lax.all_to_all(spread, "col", split_axis=1, concat_axis=0, tiled=True)
+    quarter = _spread_ports(spread, "col", 1, 0)
     quarter = quarter.reshape(col_count * child_rows, cols_here)
     quarter_blocks = quarter.shape[0] // BLK
     capacity = quarter_blocks // row_count

time: 1220 us -> 1220 us (level)
  waiting for transfers between devices: 825 us -> 773 us
  local copies, waits for them, and re-layouts: 197 us -> 230 us
  starting transfers between devices: 17.1 us -> 31.6 us
    all_to_all x1 -> x0, waiting for transfers between devices: 357 us -> none  [body(): lax.all_to_all(spread, 'col', split_axis=1, concat_axis=0, tiled=True)]
    ppermute x0 -> x7, waiting for transfers between devices: none -> 224 us  [_spread_ports(): front = lax.ppermute(front, mesh_name, val2)]
    psum x3, waiting for transfers between devices: 300 us -> 409 us  [broadcast(): return lax.psum(kept, axis)]
    all_to_all x1, waiting for transfers between devices: 168 us -> 139 us  [body(): lax.all_to_all(outgoing, 'row', split_axis=0, concat_axis=0, tiled=True)]
    ppermute x0 -> x7, local copies, waits for them, and re-layouts: none -> 18.4 us  [_spread_ports(): front = lax.ppermute(front, mesh_name, val2)]
    all_to_all x1 -> x0, local copies, waits for them, and re-layouts: 16.4 us -> none  [body(): lax.all_to_all(spread, 'col', split_axis=1, concat_axis=0, tiled=True)]
    dynamic_update_slice x0 -> x8, local copies, waits for them, and re-layouts: none -> 15 us  [_spread_ports(): lax.dynamic_update_slice_in_dim(heard, front, (z2 ^ t) * state_now, axis=...]
    dynamic_slice x0 -> x2, local copies, waits for them, and re-layouts: none -> 12.7 us  [_spread_ports(): lax.dynamic_slice_in_dim(z_in, (z2 ^ t) * k_now, k_now, axis=ndim_at)]
  transfers between devices with their start and end apart: 5 -> 11, of which waited for: 5 -> 8; matrix products, arithmetic and copies ran while one was open for 1% -> 5% of each run, Pallas kernels for 0% -> 0%
where the time goes in v1:
time: 1220 us; the launch traced here: 1210 us
  waiting for transfers between devices  773 us (63%)
  local copies, waits for them, and re-layouts  230 us (19%)
  other arithmetic  103 us (8%)
  matrix products  52.7 us (4%)
  starting transfers between devices  31.6 us (3%)
  between operations  15.2 us (1%)
    psum x3, waiting for transfers between devices, broadcast(): return lax.psum(kept, axis)  409 us
    ppermute x7, waiting for transfers between devices, _spread_ports(): front = lax.ppermute(front, mesh_name, val2)  224 us
    all_to_all x1, waiting for transfers between devices, body(): lax.all_to_all(outgoing, 'row', split_axis=0, concat_axis=0, tiled=True)  139 us
    unnamed x25, local copies, waits for them, and re-layouts  37.1 us
    another operation x6, other arithmetic, body(): factor = jnp.linalg.cholesky(diagonal_block)  34 us
    gather x2, local copies, waits for them, and re-layouts, body(): jnp.take(children.reshape(child_rows, window_blocks, BLK), inverse_cols,...  31.4 us
    reshape x2, local copies, waits for them, and re-layouts, body(): assembled = front_window + added.reshape(rows_here, cols_here)  26.3 us
  transfers between devices with their start and end apart: 11, of which 8 were waited for; matrix products, arithmetic and copies ran while one was open for 5% of the time, Pallas kernels for 0%

profile of v1, /device:TPU:0, one launch (start us, length us, event | category | flops | bytes accessed | tf_op | source)
XLA Modules:
  0.0 1205.1 jit_solution(18062723308142882122)
XLA Ops:
  8.5 17.6 %copy.44 = f32[2048,2048]{0,1:T(8,128)} copy(f32[2048,2048]{1,0:T(8,128)} %param.5) | data formatting | bytes 33554432 | tf_op args[1]
  26.1 17.6 %copy.45 = f32[2048,16,128]{2,0,1:T(8,128)} copy(f32[2048,16,128]{0,2,1:T(8,128)} %bitcast.61) | data formatting | bytes 33554432 | tf_op jit(solution)/shard_map/reshape | solution.py:45
  43.7 13.8 %gather_fusion = f32[16,2048,128]{2,1,0:T(8,128)} fusion(f32[2048,16,128]{2,0,1:T(8,128)} %copy.45, s32[1024]{0:T(1024)S(1)} %pad_clamp_fusion.1), kind=kCustom, calls=%fused_computation | custom fusion | bytes 33554496 | tf_op jit(solution)/shard_map/jit(_take)/gather | solution.py:45
  57.5 17.6 %copy.46 = f32[2048,16,128]{0,2,1:T(8,128)} copy(f32[2048,16,128]{2,0,1:T(8,128)} %bitcast.60) | data formatting | bytes 33554432 | tf_op jit(solution)/shard_map/jit(_take)/gather | solution.py:45
  75.4 11.4 bitcast_select_fusion.1
  86.9 10.9 constant_dynamic-slice_fusion.1
  119.9 117.2 %collective-permute-done.1 = f32[2048,1,256]{0,2,1:T(8,128)} collective-permute-done((f32[2048,1,256]{0,2,1:T(8,128)}, f32[2048,1,256]{0,2,1:T(8,128)}, u32[]{:S(2)}, u32[]{:S(2)}) %collective-permute-start.1) | collective-permute-done | bytes 2097184 | tf_op jit(solution)/shard_map/ppermute | solution.py:24
  243.2 38.3 %collective-permute-done.2 = f32[2048,1,256]{0,2,1:T(8,128)} collective-permute-done((f32[2048,1,256]{0,2,1:T(8,128)}, f32[2048,1,256]{0,2,1:T(8,128)}, u32[]{:S(2)}, u32[]{:S(2)}) %collective-permute-start.2) | collective-permute-done | bytes 2097184 | tf_op jit(solution)/shard_map/ppermute | solution.py:24
  290.3 39.7 %collective-permute-done.5 = f32[2048,1,256]{0,2,1:T(8,128)} collective-permute-done((f32[2048,1,256]{0,2,1:T(8,128)}, f32[2048,1,256]{0,2,1:T(8,128)}, u32[]{:S(2)}, u32[]{:S(2)}) %collective-permute-start.5) | collective-permute-done | bytes 2097184 | tf_op jit(solution)/shard_map/ppermute | solution.py:24
  345.0 29.0 %collective-permute-done.6 = f32[2048,1,256]{0,2,1:T(8,128)} collective-permute-done((f32[2048,1,256]{0,2,1:T(8,128)}, f32[2048,1,256]{0,2,1:T(8,128)}, u32[]{:S(2)}, u32[]{:S(2)}) %collective-permute-start.6) | collective-permute-done | bytes 2097184 | tf_op jit(solution)/shard_map/ppermute | solution.py:24
  377.4 15.6 %gather_fusion.1 = f32[128,128,256]{2,1,0:T(8,128)} fusion(f32[128,128,256]{2,1,0:T(8,128)} %bitcast.6, s32[1024]{0:T(1024)S(1)} %pad_clamp_fusion), kind=kCustom, calls=%fused_computation.1 | custom fusion | bytes 33554944 | tf_op jit(solution)/shard_map/jit(_take)/gather | solution.py:56
  393.0 12.2 %bitcast_select_fusion = f32[2,8192,256]{2,1,0:T(8,128)} fusion(pred[2,8192]{1,0:T(4,128)(4,1)S(1)} %bitcast.62, f32[2,8192,256]{2,1,0:T(8,128)} %bitcast.58), kind=kLoop, calls=%fused_computation.8 | loop fusion | flops 4194304 | bytes 33570816 | tf_op jit(solution)/shard_map/jit(_take)/select_n | solution.py:56
  405.2 9.7 all-to-all-start
  414.9 11.8 all-reduce.5.cloned.1.call-start
  426.7 12.6 %copy.55 = f32[12288,256]{0,1:T(8,128)} copy(f32[12288,256]{1,0:T(8,128)} %param.4) | data formatting | bytes 25165824 | tf_op args[0]
  441.3 139.0 %all-to-all-done = f32[2,8192,256]{2,1,0:T(8,128)} async-done(((f32[2,8192,256]{2,1,0:T(8,128)}), f32[2,8192,256]{2,1,0:T(8,128)}, u32[]{:S(2)}, u32[]{:S(2)}) %all-to-all-start) | async-done | bytes 16777248 | tf_op jit(solution)/shard_map/all_to_all | solution.py:58
  580.3 18.2 %reshape.122 = f32[128,32768]{1,0:T(8,128)} reshape(f32[2,8192,256]{2,1,0:T(8,128)} %all-to-all-done) | data formatting | bytes 33554432 | tf_op jit(solution)/shard_map/reshape | solution.py:67
  598.5 14.1 %fusion.17 = f32[96,32768]{1,0:T(8,128)} fusion(f32[128,32768]{1,0:T(8,128)} %reshape.122, s32[128]{0:T(128)S(1)} %and_select_fusion), kind=kOutput, calls=%fused_computation.46 | convolution fusion | flops 4831850496 | bytes 29360640 | tf_op jit(solution)/shard_map/sp,sk->pk/dot_general | solution.py:64
  612.6 13.6 %reshape.123 = f32[12288,256]{1,0:T(8,128)} reshape(f32[96,32768]{1,0:T(8,128)} %fusion.17) | data formatting | bytes 25165824 | tf_op jit(solution)/shard_map/reshape | solution.py:70
  626.3 12.6 %copy.56 = f32[12288,256]{0,1:T(8,128)} copy(f32[12288,256]{1,0:T(8,128)} %reshape.123) | data formatting | bytes 25165824 | tf_op jit(solution)/shard_map/reshape | solution.py:70
  638.9 18.5 %broadcast_select_fusion = (f32[12288,256]{0,1:T(8,128)}, f32[12288,256]{0,1:T(8,128)}) fusion(pred[]{:T(512)S(6)} %eq.31, f32[12288,256]{0,1:T(8,128)} %copy.55, f32[12288,256]{0,1:T(8,128)} %copy.56), kind=kLoop, calls=%fused_computation.13 | loop fusion | flops 6291456 | bytes 50331648 | tf_op jit(solution)/shard_map/jit(_where)/select_n | solution.py:30
  657.5 362.1 %all-reduce.5.cloned.1.call-done = f32[12288,256]{0,1:T(8,128)} async-done(((f32[12288,256]{0,1:T(8,128)}), f32[12288,256]{0,1:T(8,128)}) %all-reduce.5.cloned.1.call-update) | async-done | bytes 12582928 | tf_op jit(solution)/shard_map/psum | solution.py:31
  1021.5 23.9 %all-reduce.7.cloned.1.call-done = f32[256,256]{0,1:T(8,128)} async-done(((f32[256,256]{0,1:T(8,128)}), f32[256,256]{0,1:T(8,128)}) %all-reduce.7.cloned.1.call-update) | async-done | bytes 262160 | tf_op jit(solution)/shard_map/psum | solution.py:31
  1047.4 11.7 cholesky.49
  1059.2 9.8 custom-call.15
  1069.5 11.7 cholesky.103
  1088.0 19.7 %custom-call.16 = f32[2,128,128]{1,2,0:T(8,128)S(1)} custom-call(f32[2,128,128]{2,1,0:T(8,128)S(1)} %get-tuple-element.16), custom_call_target="InvertDiagBlocksLowerTriangular" | custom-call | tf_op jit(solution)/shard_map/jit(_solve_triangular)/triangular_solve | solution.py:76
  1108.6 14.1 %fusion.3 = f32[12288,256]{0,1:T(8,128)S(1)} fusion(f32[12288,256]{0,1:T(8,128)} %all-reduce.5.cloned.1.call-done, f32[128,256]{1,0:T(8,128)S(1)} %fusion.13, f32[128,256]{1,0:T(8,128)S(1)} %fusion.10), kind=kOutput, calls=%fused_computation.19 | convolution fusion | flops 9663741952 | bytes 25427968 | tf_op jit(solution)/shard_map/dot_general | solution.py:77
  1127.5 9.7 slice.79
  1139.1 23.4 %all-reduce.9.cloned.1.call-done = f32[256,256]{0,1:T(8,128)} async-done(((f32[256,256]{0,1:T(8,128)}), f32[256,256]{0,1:T(8,128)}) %all-reduce.9.cloned.1.call-update) | async-done | bytes 262160 | tf_op jit(solution)/shard_map/psum | solution.py:31
  1162.5 23.1 %fusion = f32[12288,256]{0,1:T(8,128)} fusion(f32[12288,256]{0,1:T(8,128)} %get-tuple-element.42, f32[256,256]{0,1:T(8,128)} %all-reduce.9.cloned.1.call-done, f32[256,256]{0,1:T(8,128)S(1)} %slice_select_fusion, f32[12032,256]{0,1:T(8,128)} %slice.79, pred[256]{0:T(512)(128)(4,1)S(1)} %get-tuple-element.56, pred[12288]{0:T(1024)(128)(4,1)S(1)} %add_compare_fusion, ...), kind=kOutput, calls=%fused_computation.10 | convolution fusion | flops 9682550784 | bytes 38023680 | tf_op jit(solution)/shard_map/dot_general | solution.py:84
  1185.5 12.6 %copy.65 = f32[12288,256]{1,0:T(8,128)} copy(f32[12288,256]{0,1:T(8,128)} %fusion) | data formatting | bytes 25165824 | tf_op jit(solution)/shard_map/jit(_where)/select_n | solution.py:88
  (118 shorter events, 81.0 us)
Async XLA Ops:
  6.5 0.7 copy-start
  6.5 112.7 %sort.37.cloned.1.call-start = ((), (), s32[]{:S(2)}) async-start(), calls=%async_computation.4 | async-start | bytes 6176 | tf_op jit(solution)/shard_map/jit(argsort)/sort | solution.py:54
  86.9 21.8 %copy-start.2 = (s32[2,128]{1,0:T(2,128)S(1)}, s32[2,128]{1,0:T(2,128)}, u32[]{:S(2)}) copy-start(s32[2,128]{1,0:T(2,128)} %param.6) | copy-start | bytes 3076
  97.8 6.0 collective-permute-start
  98.3 138.9 %collective-permute-start.1 = (f32[2048,1,256]{0,2,1:T(8,128)}, f32[2048,1,256]{0,2,1:T(8,128)}, u32[]{:S(2)}, u32[]{:S(2)}) collective-permute-start(f32[2048,1,256]{0,2,1:T(8,128)} %get-tuple-element.50), channel_id=1, source_target_pairs={{0,2},{1,3},{2,0},{3,1},{4,6},{5,7},{6,4},{7,5},{8,10},{9,11},{10,... | collective-permute-start | bytes 6291464 | tf_op jit(solution)/shard_map/ppermute | solution.py:24
  100.9 180.6 %collective-permute-start.2 = (f32[2048,1,256]{0,2,1:T(8,128)}, f32[2048,1,256]{0,2,1:T(8,128)}, u32[]{:S(2)}, u32[]{:S(2)}) collective-permute-start(f32[2048,1,256]{0,2,1:T(8,128)} %get-tuple-element.49), channel_id=1, source_target_pairs={{0,3},{1,2},{2,1},{3,0},{4,7},{5,6},{6,5},{7,4},{8,11},{9,10},{10,... | collective-permute-start | bytes 6291464 | tf_op jit(solution)/shard_map/ppermute | solution.py:24
  101.0 183.5 %collective-permute-start.3 = (f32[2048,1,256]{0,2,1:T(8,128)}, f32[2048,1,256]{0,2,1:T(8,128)}, u32[]{:S(2)}, u32[]{:S(2)}) collective-permute-start(f32[2048,1,256]{0,2,1:T(8,128)} %get-tuple-element.48), channel_id=1, source_target_pairs={{0,4},{1,5},{2,6},{3,7},{4,0},{5,1},{6,2},{7,3},{8,12},{9,13},{10,... | collective-permute-start | bytes 6291464 | tf_op jit(solution)/shard_map/ppermute | solution.py:24
  103.8 183.6 %collective-permute-start.4 = (f32[2048,1,256]{0,2,1:T(8,128)}, f32[2048,1,256]{0,2,1:T(8,128)}, u32[]{:S(2)}, u32[]{:S(2)}) collective-permute-start(f32[2048,1,256]{0,2,1:T(8,128)} %get-tuple-element.47), channel_id=1, source_target_pairs={{0,5},{1,4},{2,7},{3,6},{4,1},{5,0},{6,3},{7,2},{8,13},{9,12},{10,... | collective-permute-start | bytes 6291464 | tf_op jit(solution)/shard_map/ppermute | solution.py:24
  103.8 1.3 copy-start.8
  105.1 224.9 %collective-permute-start.5 = (f32[2048,1,256]{0,2,1:T(8,128)}, f32[2048,1,256]{0,2,1:T(8,128)}, u32[]{:S(2)}, u32[]{:S(2)}) collective-permute-start(f32[2048,1,256]{0,2,1:T(8,128)} %get-tuple-element.46), channel_id=1, source_target_pairs={{0,6},{1,7},{2,4},{3,5},{4,2},{5,3},{6,0},{7,1},{8,14},{9,15},{10,... | collective-permute-start | bytes 6291464 | tf_op jit(solution)/shard_map/ppermute | solution.py:24
  111.7 6.0 copy-start.7
  237.2 136.9 %collective-permute-start.6 = (f32[2048,1,256]{0,2,1:T(8,128)}, f32[2048,1,256]{0,2,1:T(8,128)}, u32[]{:S(2)}, u32[]{:S(2)}) collective-permute-start(f32[2048,1,256]{0,2,1:T(8,128)} %get-tuple-element.45), channel_id=1, source_target_pairs={{0,7},{1,6},{2,5},{3,4},{4,3},{5,2},{6,1},{7,0},{8,15},{9,14},{10,... | collective-permute-start | bytes 6291464 | tf_op jit(solution)/shard_map/ppermute | solution.py:24
  332.9 7.7 copy-start.4
  332.9 9.2 copy-start.5
  332.9 10.7 copy-start.6
  405.2 175.0 %all-to-all-start = ((f32[2,8192,256]{2,1,0:T(8,128)}), f32[2,8192,256]{2,1,0:T(8,128)}, u32[]{:S(2)}, u32[]{:S(2)}) async-start(f32[2,8192,256]{2,1,0:T(8,128)} %bitcast_select_fusion), calls=%async_computation | async-start | bytes 33554432 | tf_op jit(solution)/shard_map/all_to_all | solution.py:58
  414.9 604.7 %all-reduce.5.cloned.1.call-start = ((), (), s32[]{:S(2)}) async-start(), calls=%async_computation.1 | async-start | bytes 25165824 | tf_op jit(solution)/shard_map/psum | solution.py:31
  426.7 12.6 %copy-start.9 = (s32[2,128]{1,0:T(2,128)S(1)}, s32[2,128]{1,0:T(2,128)}, u32[]{:S(2)}) copy-start(s32[2,128]{1,0:T(2,128)} %get-tuple-element.7) | copy-start | bytes 3076
  657.5 387.9 %all-reduce.7.cloned.1.call-start = ((), (), s32[]{:S(2)}) async-start(), calls=%async_computation.2 | async-start | bytes 524288 | tf_op jit(solution)/shard_map/psum | solution.py:31
  1021.3 141.1 %all-reduce.9.cloned.1.call-start = ((), (), s32[]{:S(2)}) async-start(), calls=%async_computation.3 | async-start | bytes 524288 | tf_op jit(solution)/shard_map/psum | solution.py:31
  1122.7 4.8 copy-start.3
  1162.5 35.7 %copy-start.1 = (s32[2,16]{1,0:T(2,128)S(1)}, s32[2,16]{1,0:T(2,128)}, u32[]{:S(2)}) copy-start(s32[2,16]{1,0:T(2,128)} %param.7) | copy-start | bytes 388
Sparse Core Ops, SparseCore 0:
  110.0 2.0 sort.39.cloned.1.call-done
  657.6 362.0 all-reduce.4
  1021.9 23.3 all-reduce.6
  1139.1 23.2 all-reduce.8
  (1 shorter events, 0.0 us)
